TPU v7x, 32 devices: a whole 2x2x4 slice. The times are simulated.
32 devices in a mesh: section: 2 (over x), seq: 4 (over y, core), dp: 4 (over z).
Axes of the slice: x: 2, y: 2, z: 4, core: 2. Of those that a mesh axis runs over, the one named last changes fastest.
Arguments:
- frozen_queries: bfloat16 [2, 4, 512, 4096], P('section', 'dp', 'seq'), may hold values from -128 to 128
- key_value_pairs: bfloat16 [2, 4, 512, 1024], P('section', 'dp', 'seq'), may hold values from -8 to 8
- adapter_input: bfloat16 [2, 4, 512, 64], P('section', 'dp', 'seq'), may hold values from -6 to 6
- adapter_up_matrix: bfloat16 [2, 64, 4096], P('section', None, 'seq'), may hold values from -0.75 to 0.75
- upstream: bfloat16 [2, 4, 512, 4096], P('section', 'dp', 'seq'), may hold values from -6 to 6
- document_index: int32 [2, 4, 512], P('section', 'dp'), may hold values from 0 to 15, as said below
Outputs:
- query_gradient: bfloat16 [2, 4, 512, 4096], P('section', 'dp', 'seq')
- key_value_gradient: bfloat16 [2, 4, 512, 1024], P('section', 'dp', 'seq')
- adapter_input_gradient: bfloat16 [2, 4, 512, 64], P('section', 'dp', 'seq')
- adapter_up_gradient: float32 [2, 64, 4096], P('section', 'dp', 'seq')
Inputs may be any that keep to these rules, and one draw needn't show every extreme that they name: `document_index`: along each pack the numbers never fall; every number appears; every document spans at most 64 positions, and one document of each pack spans exactly that many.
All inputs are finite; a program needn't handle non-finite values.
Results may differ from a plain program's by a relative error of at most 0.014.
Values may be sent and summed in bfloat16 or wider, within the bound.
No kernel may reach another device: no remote copies, remote signals or barrier semaphores. Data moves between devices by JAX's collectives and lax.ppermute only.
A program may use at most 64 MiB of HBM per device.

v0:
```python
import functools
import math
from types import SimpleNamespace

import jax
import jax.numpy as jnp
from jax import lax
from jax.experimental import pallas as pl
from jax.experimental.pallas import tpu as pltpu
from jax.sharding import PartitionSpec as P

QUERY_HEADS = 32
HK = 4
HEAD_SIZE = 128
PAIR = 2 * HEAD_SIZE
SCALE = 1.0 / math.sqrt(HEAD_SIZE)
SPAN_PARTS = 8

WHOLE, FRONT, BACK, FINISH = range(4)
PHASE_NAMES = ("whole", "front", "back", "finish")
IN = "_in"
DQ = "dq_out"
DQ_IN = DQ + IN
SHARES = ["share" + str(index) for index in range(64)]
PENDING = ["pending" + str(index) for index in range(2)]
TERMS = ["term_in" + str(index) for index in range(64)]

VMEM = pl.BlockSpec(memory_space=pltpu.VMEM)
HBM = pl.BlockSpec(memory_space=pltpu.HBM)
LIMIT = 16 * 1024 * 1024
BLOCKS = 2


def passed_along(value, axis, steps):
    count = lax.axis_size(axis)
    pairs = [(source, (source + steps) % count) for source in range(count)]
    return lax.ppermute(value, axis, pairs)


def partner(place, away, count):
    if count & (count - 1) == 0:
        return place ^ away
    return (place + away) % count


def dot(left, right, left_dim, right_dim):
    return lax.dot_general(
        left, right, (((left_dim,), (right_dim,)), ((), ())), preferred_element_type=jnp.float32
    )


def chunk_at(step, chunks):
    return lax.rem(lax.axis_index("seq") + (2 * chunks - 1 - step), chunks)


def split_kernel(steps, chunks, bundled, upstream, own, matrix, *rest):
    rest = list(rest)
    sems = rest.pop()
    if steps[0] > 0:
        rest.pop(0)
    rows = upstream.shape[0]
    width = upstream.shape[1] // chunks
    copies = []

    def send(source, target):
        copies.append(pltpu.make_async_copy(source, target, sems.at[len(copies)]))
        copies[-1].start()

    for step in steps:
        start = pl.multiple_of(chunk_at(step, chunks) * width, HEAD_SIZE)
        columns = pl.ds(start, width)
        if step < chunks - 1:
            send(upstream.at[:, columns], rest.pop(0))
        else:
            send(upstream.at[pl.ds(0, rows // BLOCKS), columns], rest.pop(0))
            send(upstream.at[pl.ds(rows // BLOCKS, rows // BLOCKS), columns], rest.pop(0))
    if steps[0] > 0:
        send(matrix, rest.pop(0))
    if bundled > 0:
        bundle = rest.pop(0)
        send(own.at[pl.ds(rows - bundled, bundled)], bundle.at[pl.ds(0, bundled)])
        send(matrix, bundle.at[pl.ds(bundled, matrix.shape[0])])
    for copy in copies:
        copy.wait()


def split_columns(steps, chunks, bundled, upstream, own, matrix, after):
    rows, columns = upstream.shape
    shapes = []
    for step in steps:
        if step < chunks - 1:
            shapes.append(jax.ShapeDtypeStruct((rows, columns // chunks), upstream.dtype))
        else:
            half = jax.ShapeDtypeStruct((rows // BLOCKS, columns // chunks), upstream.dtype)
            shapes += [half] * BLOCKS
    if steps[0] > 0:
        shapes.append(jax.ShapeDtypeStruct(matrix.shape, matrix.dtype))
    if bundled > 0:
        shapes.append(jax.ShapeDtypeStruct((bundled + matrix.shape[0], own.shape[1]), own.dtype))
    operands = [
        pltpu.with_memory_space_constraint(array, pltpu.HBM) for array in (upstream, own, matrix)
    ] + after
    return list(
        pl.pallas_call(
            functools.partial(split_kernel, steps, chunks, bundled),
            in_specs=[HBM] * 3 + [VMEM] * len(after),
            out_specs=[VMEM] * len(shapes),
            out_shape=shapes,
            scratch_shapes=[pltpu.SemaphoreType.DMA((len(shapes) + 1,))],
            compiler_params=pltpu.CompilerParams(vmem_limit_bytes=LIMIT),
            cost_estimate=pl.CostEstimate(
                flops=0, bytes_accessed=4 * rows * columns, transcendentals=0
            ),
            name="split_columns",
        )(*operands)
    )


def stacked(array, rows):
    heads = array.shape[1] // HEAD_SIZE
    parts = [array[rows, head * HEAD_SIZE : (head + 1) * HEAD_SIZE] for head in range(heads)]
    return jnp.concatenate(parts, axis=0)


def softmax_block(query_stack, key_window, hidden):
    copies = query_stack.shape[0] // hidden.shape[1]
    scores = dot(key_window, query_stack, 1, 1) * SCALE
    scores += jnp.concatenate([hidden] * copies, axis=1)
    shifted = jnp.exp(scores - jnp.max(scores, axis=0, keepdims=True))
    return shifted * (1.0 / jnp.sum(shifted, axis=0, keepdims=True))


def block_grads(probs, key_window, value_window, cot_stack):
    dprobs = dot(value_window, cot_stack, 1, 1)
    deltas = jnp.sum(probs * dprobs, axis=0, keepdims=True)
    dscores = (probs * (dprobs - deltas)).astype(jnp.bfloat16)
    return dscores, (dot(dscores, key_window, 0, 0) * SCALE).astype(jnp.bfloat16)


def pair_terms(index, block, total, dscores, probs, query_stack, cot_stack):
    key_term = dot(dscores, query_stack, 1, 0) * SCALE
    value_term = dot(probs.astype(jnp.bfloat16), cot_stack, 1, 0)
    term = jnp.concatenate([key_term, value_term], axis=1)
    start = index * block
    rest = total - term.shape[0] - start
    if start > 0:
        term = jnp.concatenate([jnp.zeros((start, PAIR), jnp.float32), term], axis=0)
    if rest > 0:
        term = jnp.concatenate([term, jnp.zeros((rest, PAIR), jnp.float32)], axis=0)
    return term


def padded(grad, index, block):
    blank = jnp.zeros((block, grad.shape[1]), grad.dtype)
    return jnp.concatenate([grad if place == index else blank for place in range(BLOCKS)], axis=0)


def chunk_kernel(step, phase, chunks, up_row, pending, names, *refs):
    refs = SimpleNamespace(**dict(zip(names, refs)))
    first = step == 0
    fq, at, up, cot = refs.fq, refs.at, refs.up, refs.cot
    halo, own, bias = refs.halo, refs.own, refs.bias
    rows = fq.shape[0]
    block = rows // BLOCKS
    rank = at.shape[0]
    window = bias.shape[0] // BLOCKS
    span = window - block
    width = fq.shape[1] // chunks
    heads = width // HEAD_SIZE

    def columns_of(at_step):
        return pl.ds(pl.multiple_of(chunk_at(at_step, chunks) * width, HEAD_SIZE), width)

    copies = []
    for index, (at_step, start, count) in enumerate(pending):
        target = refs.dq_out.at[pl.ds(start, count), columns_of(at_step)]
        copies.append(pltpu.make_async_copy(getattr(refs, PENDING[index]), target, refs.sems.at[index]))
        copies[-1].start()

    chunk = chunk_at(step, chunks)
    place = lax.div(chunk, chunks // HK) if chunks > HK else chunk
    key_columns = pl.ds(pl.multiple_of(place * PAIR, HEAD_SIZE), HEAD_SIZE)
    value_columns = pl.ds(pl.multiple_of(place * PAIR + HEAD_SIZE, HEAD_SIZE), HEAD_SIZE)
    slot = pl.ds(pl.multiple_of(chunk * PAIR, HEAD_SIZE), PAIR)
    adapter = at[...]
    matrix = up[up_row : up_row + rank]

    if phase in (WHOLE, FRONT, BACK):
        keys = jnp.concatenate([halo[:span, key_columns], own[:, key_columns]], axis=0)
        values = jnp.concatenate([halo[:span, value_columns], own[:, value_columns]], axis=0)
    if phase in (WHOLE, FRONT):
        queries = fq[:, columns_of(step)].astype(jnp.float32) + dot(adapter, matrix, 0, 0)
        queries = queries.astype(jnp.bfloat16)
        query_stacks, probs = {}, {}
        for index in range(BLOCKS):
            query_stacks[index] = stacked(queries, slice(index * block, (index + 1) * block))
            probs[index] = softmax_block(
                query_stacks[index],
                keys[index * block : index * block + window],
                bias[index * window : (index + 1) * window],
            )
    else:
        query_stacks = {1: refs.query_stack[...]}
        probs = {1: refs.probs[...]}
    if phase == FRONT:
        refs.query_stack_out[...] = query_stacks[1]
        refs.probs_out[...] = probs[1]

    blocks = {WHOLE: (0, 1), FRONT: (0,), BACK: (1,), FINISH: (1,)}[phase]
    cot_stacks, dscores = {}, {}
    for index in blocks:
        start = index * block if phase == WHOLE else 0
        cot_stacks[index] = stacked(cot, slice(start, start + block))
        if phase == FINISH:
            dscores[index] = refs.dscores[...]
            continue
        low = index * block
        dscores[index], grad_stack = block_grads(
            probs[index], keys[low : low + window], values[low : low + window], cot_stacks[index]
        )
        for head in range(heads):
            columns = slice(head * HEAD_SIZE, (head + 1) * HEAD_SIZE)
            part = grad_stack[head * block : (head + 1) * block]
            refs.grad_out[start : start + block, columns] = part
    grad = (refs.pending1 if phase == FINISH else refs.grad_out)[...]
    if phase != WHOLE:
        grad = padded(grad, blocks[0], block)

    if phase != FINISH:
        weight_term = dot(adapter, grad, 1, 0)
        received_sum = jnp.zeros_like(weight_term) if first else refs.weight_sum[...]
        for name in names:
            if name in TERMS:
                received_sum += getattr(refs, name)[...].astype(jnp.float32)
    if phase == WHOLE:
        refs.weight_out[...] = received_sum
        refs.term_out[...] = weight_term.astype(jnp.bfloat16)
    elif phase == FRONT:
        refs.weight_out[...] = weight_term + received_sum
    elif phase == BACK:
        refs.dscores_out[...] = dscores[1]
        total = refs.total
        total[...] = (weight_term + received_sum).astype(jnp.bfloat16)
        shares = [name for name in names if name in SHARES]
        share_rows = rank // len(shares)
        for away, name in enumerate(shares):
            target = partner(lax.axis_index("dp"), away, len(shares))
            start = pl.multiple_of(target * share_rows, share_rows)
            getattr(refs, name)[...] = total[pl.ds(start, share_rows)]

    if phase != BACK:
        input_term = dot(matrix, grad, 1, 1)
        if not first:
            input_term += refs.input_sum[...]
        refs.input_out[...] = input_term.astype(refs.input_out.dtype)
        pair_total = refs.own_part[...] if phase == FINISH else 0.0
        for index in blocks:
            pair_total += pair_terms(
                index,
                block,
                span + rows,
                dscores[index],
                probs[index],
                query_stacks[index],
                cot_stacks[index],
            )
        if phase != FINISH:
            refs.halo_out[:, slot] = pair_total[:span].astype(refs.halo_out.dtype)
        if phase == FRONT:
            refs.own_part_out[...] = pair_total
        else:
            refs.own_out[:, slot] = pair_total[span:]
        if hasattr(refs, "pair_out"):
            low = rows - span
            refs.pair_out[:low] = refs.own_out[:low].astype(jnp.bfloat16)
            total = refs.own_out[low:] + refs.halo_back[...].astype(jnp.float32)
            refs.pair_out[low:] = total.astype(jnp.bfloat16)
    for copy in copies:
        copy.wait()


def chunk_step(step, phase, chunks, up_row, inputs, carried, pending, terms):
    fq, bias, at = inputs.fq, inputs.bias, inputs.at
    rows, columns = fq.shape
    width = columns // chunks
    heads = width // HEAD_SIZE
    rank = at.shape[0]
    block = rows // BLOCKS
    window = bias.shape[0] // BLOCKS
    span = window - block
    halo_type = jnp.bfloat16 if chunks == HK else jnp.float32

    outputs = {}
    if pending:
        outputs.update(dq_out=((rows, columns), jnp.bfloat16))
    if phase in (WHOLE, FRONT):
        outputs.update(halo_out=((span, chunks * PAIR), halo_type))
    if phase in (WHOLE, FINISH):
        outputs.update(own_out=((rows, chunks * PAIR), jnp.float32))
    handed = [name for name in outputs if hasattr(carried, name)]
    if phase != BACK:
        kind = jnp.bfloat16 if phase == FINISH else jnp.float32
        outputs.update(input_out=((rank, rows), kind))
    if phase != FINISH:
        grad_rows = rows if phase == WHOLE else block
        outputs.update(grad_out=((grad_rows, width), jnp.bfloat16))
    if phase == WHOLE:
        outputs.update(term_out=((rank, width), jnp.bfloat16))
    if phase in (WHOLE, FRONT):
        outputs.update(weight_out=((rank, width), jnp.float32))
    if phase == FRONT:
        outputs.update(query_stack_out=((heads * block, HEAD_SIZE), jnp.bfloat16))
        outputs.update(probs_out=((window, heads * block), jnp.float32))
        outputs.update(own_part_out=((span + rows, PAIR), jnp.float32))
    if phase == BACK:
        outputs.update(dscores_out=((window, heads * block), jnp.bfloat16))
        packs = lax.axis_size("dp")
        for away in range(packs):
            outputs[SHARES[away]] = ((rank // packs, width), jnp.bfloat16)

    operands = dict(vars(inputs))
    if hasattr(inputs, "halo_back"):
        outputs.update(pair_out=((rows, chunks * PAIR), jnp.bfloat16))
    aliases = {}
    for name in handed:
        aliases[len(operands)] = list(outputs).index(name)
        operands[name + IN] = getattr(carried, name)
    if step > 0 and phase != BACK:
        operands.update(input_sum=carried.input_out)
    if step > 0 and phase != FINISH:
        operands.update(weight_sum=carried.weight_out)
    if phase in (BACK, FINISH):
        operands.update(query_stack=carried.query_stack_out)
        operands.update(probs=carried.probs_out)
    if phase == FINISH:
        operands.update(own_part=carried.own_part_out)
        operands.update(dscores=carried.dscores_out)
    for index, (_, _, array) in enumerate(pending):
        operands[PENDING[index]] = array
    for index, term in enumerate(terms):
        operands[TERMS[index]] = term
    scratch = dict(
        total=pltpu.VMEM((rank, width), jnp.bfloat16),
        sems=pltpu.SemaphoreType.DMA((2,)),
    )
    names = list(operands) + list(outputs) + list(scratch)
    places = [(at_step, start, array.shape[0]) for at_step, start, array in pending]
    results = pl.pallas_call(
        functools.partial(chunk_kernel, step, phase, chunks, up_row, places, names),
        in_specs=[HBM if name == DQ_IN else VMEM for name in operands],
        out_specs=[HBM if name == DQ else VMEM for name in outputs],
        out_shape=[jax.ShapeDtypeStruct(*shape) for shape in outputs.values()],
        scratch_shapes=list(scratch.values()),
        input_output_aliases=aliases,
        compiler_params=pltpu.CompilerParams(vmem_limit_bytes=LIMIT),
        cost_estimate=pl.CostEstimate(
            flops=heads * 10 * rows * window * HEAD_SIZE,
            bytes_accessed=8 * rows * width,
            transcendentals=heads * rows * window,
        ),
        name="chunk_" + PHASE_NAMES[phase],
    )(*operands.values())
    vars(carried).update(zip(outputs, results))


def per_device(
    frozen_queries, key_value_pairs, adapter_input, adapter_up_matrix, upstream, document_index
):
    chunks = lax.axis_size("seq")
    place = lax.axis_index("seq")
    rows = frozen_queries.shape[2]
    block = rows // BLOCKS
    length = document_index.shape[2]
    span = length // SPAN_PARTS
    window = span + block
    per_head = chunks // HK
    steps = tuple(range(chunks))

    pieces = []
    left = span
    while left > 0:
        pieces.append((len(pieces) + 1, min(rows, left)))
        left -= rows

    own = key_value_pairs[0, 0]
    own_matrix = adapter_up_matrix[0]
    bundled = span if len(pieces) == 1 and own_matrix.shape[1] == own.shape[1] else 0

    parts = split_columns(steps[:1], chunks, 0, upstream[0, 0], own, own_matrix, [])
    parts += split_columns(steps[1:], chunks, bundled, upstream[0, 0], own, own_matrix, parts[:1])
    cots = [passed_along(part, "section", -1) for part in parts[: chunks + 1]]
    own_matrix = parts[chunks + 1]
    if bundled > 0:
        halo = passed_along(parts[-1], "seq", 1)
        matrices, up_rows = [halo], [span]
    else:
        halo_parts = [
            passed_along(own[rows - count :], "seq", distance) for distance, count in pieces
        ]
        halo = jnp.concatenate(halo_parts[::-1], axis=0)
        matrices, up_rows = [passed_along(own_matrix, "seq", 1)], [0]
    matrices += [passed_along(own_matrix, "seq", step + 1) for step in steps[1:-1]] + [own_matrix]
    up_rows += [0] * (chunks - 1)

    numbers = jnp.concatenate([jnp.full((span,), -1, jnp.int32), document_index[0, 0]])
    numbers = lax.dynamic_slice_in_dim(numbers, place * rows, span + rows, 0)
    reach = jnp.arange(window, dtype=jnp.int32)[:, None] <= (
        jnp.arange(block, dtype=jnp.int32)[None, :] + span
    )
    bias = []
    for start in range(0, rows, block):
        seen = numbers[start : start + window, None]
        same = seen == numbers[None, start + span : start + span + block]
        bias.append(jnp.where(same & reach, 0.0, -jnp.inf))
    bias = jnp.concatenate(bias, axis=0).astype(jnp.float32)
    bias = jnp.concatenate([bias, bias], axis=1)

    inputs = SimpleNamespace(
        fq=frozen_queries[0, 0], at=adapter_input[0, 0].T, halo=halo, own=own, bias=bias
    )
    carried, terms, pending = SimpleNamespace(), [], []
    for step in steps:
        phases = (WHOLE,) if step < chunks - 1 else (FRONT, BACK)
        for phase in phases:
            taken = 0 if step < 2 else len(terms) if phase == BACK else 1
            inputs.up = matrices[step]
            inputs.cot = cots[step + (phase == BACK)]
            written = [] if phase == BACK else pending
            chunk_step(
                step, phase, chunks, up_rows[step], inputs, carried, written, terms[:taken]
            )
            terms = terms[taken:]
            if phase == BACK:
                pending.append((step, block, carried.grad_out))
            else:
                pending = [(step, 0, carried.grad_out)]
            if phase == WHOLE:
                terms.append(passed_along(carried.term_out, "seq", -(step + 1)))

    packs = lax.axis_size("dp")
    weight_share = carried.share0.astype(jnp.float32)
    for away in range(1, packs):
        pairs = [(source, partner(source, away, packs)) for source in range(packs)]
        weight_share += lax.ppermute(getattr(carried, SHARES[away]), "dp", pairs).astype(jnp.float32)

    halo_grads = carried.halo_out
    if per_head > 1:
        halo_grads = jnp.sum(halo_grads.reshape(span, HK, per_head, PAIR), axis=2)
        halo_grads = halo_grads.astype(jnp.bfloat16).reshape(span, HK * PAIR)
    backs = []
    stop = span
    for distance, count in pieces:
        backs.append(passed_along(halo_grads[stop - count : stop], "seq", -distance))
        stop -= count
    if per_head == 1 and len(pieces) == 1:
        inputs.halo_back = backs[0]
    chunk_step(
        step, FINISH, chunks, up_rows[step], inputs, carried, pending, []
    )
    if hasattr(inputs, "halo_back"):
        pair_grads = carried.pair_out
    else:
        own_grads = jnp.sum(carried.own_out.reshape(rows, HK, per_head, PAIR), axis=2)
        own_grads = own_grads.reshape(rows, HK * PAIR)
        for back in backs:
            low = rows - back.shape[0]
            own_grads = own_grads.at[low:].add(back.astype(jnp.float32))
        pair_grads = own_grads.astype(jnp.bfloat16)

    return (
        carried.dq_out[None, None],
        pair_grads[None, None],
        carried.input_out.T[None, None],
        weight_share[None],
    )


def solution(mesh):
    placed = (
        P("section", "dp", "seq", None),
        P("section", "dp", "seq", None),
        P("section", "dp", "seq", None),
        P("section", None, "seq"),
        P("section", "dp", "seq", None),
        P("section", "dp", None),
    )
    return jax.shard_map(
        per_device,
        mesh=mesh,
        in_specs=placed,
        out_specs=(
            P("section", "dp", "seq", None),
            P("section", "dp", "seq", None),
            P("section", "dp", "seq", None),
            P("section", "dp", "seq"),
        ),
        check_vma=False,
    )
```

profile of v0, /device:TPU:0, one launch (start us, length us, event | category | flops | bytes accessed | tf_op | source)
XLA Modules:
  0.0 44.7 jit_solution(15759778651656114740)
XLA Ops:
  0.6 1.0 %split_columns.2.rest_0_ = bf16[128,1024]{1,0:T(8,128)(2,1)S(1)} custom-call(bf16[128,4096]{1,0:T(8,128)(2,1)} %bitcast.36, bf16[128,1024]{1,0:T(8,128)(2,1)} %bitcast.21, bf16[64,1024]{1,0:T(8,128)(2,1)} %bitcast.38), custom_call_target="tpu_custom_call" | custom-call | bytes 2097152 | tf_op jit(solution)/shard_map/split_columns/pallas_call | solution.py:104
  1.6 3.0 %collective-permute-start.7 = (bf16[128,1024]{1,0:T(8,128)(2,1)S(1)}, bf16[128,1024]{1,0:T(8,128)(2,1)S(1)}, u32[]{:S(2)}, u32[]{:S(2)}) collective-permute-start(bf16[128,1024]{1,0:T(8,128)(2,1)S(1)} %split_columns.2.rest_0_), channel_id=1, source_target_pairs={{0,16},{16,0},{1,17},{17,1},{2,18},{18,2},{3,19},{19,3},{4,20},{20... | collective-permute-start | bytes 786440 | tf_op jit(solution)/shard_map/ppermute | solution.py:37
  4.6 2.0 %split_columns.3 = (bf16[128,1024]{1,0:T(8,128)(2,1)S(1)}, bf16[128,1024]{1,0:T(8,128)(2,1)S(1)}, bf16[64,1024]{1,0:T(8,128)(2,1)S(1)}, bf16[64,1024]{1,0:T(8,12...) custom-call(bf16[128,4096]{1,0:T(8,128)(2,1)} %bitcast.37, bf16[128,1024]{1,0:T(8,128)(2,1)} %bitcast.22, ...), custom_call_target="tpu_custom_call" | custom-call | bytes 2097152 | tf_op jit(solution)/shard_map/split_columns/pallas_call | solution.py:104
  6.7 0.6 %copy-done.3 = bf16[64,1024]{1,0:T(8,128)(2,1)} copy-done((bf16[64,1024]{1,0:T(8,128)(2,1)}, bf16[64,1024]{1,0:T(8,128)(2,1)S(1)}, u32[]{:S(2)}) %copy-start.3) | copy-done | bytes 131096
  7.3 1.5 %collective-permute-start.5 = (bf16[64,1024]{1,0:T(8,128)(2,1)S(1)}, bf16[64,1024]{1,0:T(8,128)(2,1)S(1)}, u32[]{:S(2)}, u32[]{:S(2)}) collective-permute-start(bf16[64,1024]{1,0:T(8,128)(2,1)S(1)} %get-tuple-element.48.refs_5_), channel_id=1, source_target_pairs={{0,8},{4,12},{8,0},{12,4},{1,9},{5,13},{9,1},{13,5},{2,10},{6,14},... | collective-permute-start | bytes 393224 | tf_op jit(solution)/shard_map/ppermute | solution.py:37
  8.8 0.5 %collective-permute-start.4 = (bf16[128,1024]{1,0:T(8,128)(2,1)S(1)}, bf16[128,1024]{1,0:T(8,128)(2,1)S(1)}, u32[]{:S(2)}, u32[]{:S(2)}) collective-permute-start(bf16[128,1024]{1,0:T(8,128)(2,1)S(1)} %get-tuple-element.51), channel_id=1, source_target_pairs={{0,16},{16,0},{1,17},{17,1},{2,18},{18,2},{3,19},{19,3},{4,20},{20... | collective-permute-start | bytes 786440 | tf_op jit(solution)/shard_map/ppermute | solution.py:37
  9.4 1.5 %collective-permute-start.6 = (bf16[128,1024]{1,0:T(8,128)(2,1)S(1)}, bf16[128,1024]{1,0:T(8,128)(2,1)S(1)}, u32[]{:S(2)}, u32[]{:S(2)}) collective-permute-start(bf16[128,1024]{1,0:T(8,128)(2,1)S(1)} %get-tuple-element.52), channel_id=1, source_target_pairs={{0,16},{16,0},{1,17},{17,1},{2,18},{18,2},{3,19},{19,3},{4,20},{20... | collective-permute-start | bytes 786440 | tf_op jit(solution)/shard_map/ppermute | solution.py:37
  10.9 0.1 pad_dynamic-slice_fusion
  10.9 0.1 fusion.4
  11.0 0.1 fusion.5
  11.1 0.1 fusion.2
  11.2 0.1 maximum_maximum_fusion.refs_4_
  11.3 1.2 %collective-permute-start.3 = (bf16[64,1024]{1,0:T(8,128)(2,1)S(1)}, bf16[64,1024]{1,0:T(8,128)(2,1)S(1)}, u32[]{:S(2)}, u32[]{:S(2)}) collective-permute-start(bf16[64,1024]{1,0:T(8,128)(2,1)S(1)} %get-tuple-element.48.refs_5_), channel_id=1, source_target_pairs={{0,12},{4,0},{8,4},{12,8},{1,13},{5,1},{9,5},{13,9},{2,14},{6,2},{... | collective-permute-start | bytes 393224 | tf_op jit(solution)/shard_map/ppermute | solution.py:37
  12.6 2.9 %collective-permute-done.refs_2_.refs_5_ = bf16[128,1024]{1,0:T(8,128)(2,1)S(1)} collective-permute-done((bf16[128,1024]{1,0:T(8,128)(2,1)}, bf16[128,1024]{1,0:T(8,128)(2,1)S(1)}, u32[]{:S(2)}, u32[]{:S(2)}) %collective-permute-start) | collective-permute-done | bytes 262176 | tf_op jit(solution)/shard_map/ppermute | solution.py:37
  15.5 1.3 %chunk_whole.3 = (bf16[64,1024]{1,0:T(8,128)(2,1)S(1)}, f32[128,1024]{1,0:T(8,128)S(1)}, f32[64,128]{1,0:T(8,128)S(1)}, bf16[128,1024]{1,0:T(8,128)(2,1)S(1)}, b...) custom-call(bf16[128,4096]{1,0:T(8,128)(2,1)S(1)} %bitcast.15, bf16[64,128]{1,0:T(8,128)(2,1)S(1)} %bitcast.29, ...), custom_call_target="tpu_custom_call" | custom-call | flops 167772160 | bytes 1048576 | tf_op jit(solution)/shard_map/chunk_whole/pallas_call | solution.py:348
  16.9 0.1 collective-permute-start.2
  16.9 6.6 %collective-permute-done.6.refs_6_ = bf16[128,1024]{1,0:T(8,128)(2,1)S(1)} collective-permute-done((bf16[128,1024]{1,0:T(8,128)(2,1)S(1)}, bf16[128,1024]{1,0:T(8,128)(2,1)S(1)}, u32[]{:S(2)}, u32[]{:S(2)}) %collective-permute-start.6) | collective-permute-done | bytes 262176 | tf_op jit(solution)/shard_map/ppermute | solution.py:37
  23.5 1.8 %chunk_whole.4 = (bf16[128,4096]{1,0:T(8,128)(2,1)}, bf16[64,1024]{1,0:T(8,128)(2,1)S(1)}, f32[128,1024]{1,0:T(8,128)S(1)}, f32[64,128]{1,0:T(8,128)S(1)}, bf16[...) custom-call(bf16[128,4096]{1,0:T(8,128)(2,1)S(1)} %bitcast.16, ...), custom_call_target="tpu_custom_call", output_to_operand_aliasing={{1}: (7, {}), {2}: (8, {})} | custom-call | flops 167772160 | bytes 1048576 | tf_op jit(solution)/shard_map/chunk_whole/pallas_call | solution.py:348
  25.4 1.9 %collective-permute-start.1 = (bf16[64,1024]{1,0:T(8,128)(2,1)S(1)}, bf16[64,1024]{1,0:T(8,128)(2,1)S(1)}, u32[]{:S(2)}, u32[]{:S(2)}) collective-permute-start(bf16[64,1024]{1,0:T(8,128)(2,1)S(1)} %get-tuple-element.49), channel_id=1, source_target_pairs={{0,16},{16,0},{1,17},{17,1},{2,18},{18,2},{3,19},{19,3},{4,20},{20... | collective-permute-start | bytes 393224 | tf_op jit(solution)/shard_map/ppermute | solution.py:37
  27.4 1.6 %chunk_whole.5 = (bf16[128,4096]{1,0:T(8,128)(2,1)}, bf16[64,1024]{1,0:T(8,128)(2,1)S(1)}, f32[128,1024]{1,0:T(8,128)S(1)}, f32[64,128]{1,0:T(8,128)S(1)}, bf16[...) custom-call(bf16[128,4096]{1,0:T(8,128)(2,1)S(1)} %bitcast.17, ...), custom_call_target="tpu_custom_call", output_to_operand_aliasing={{0}: (7, {}), {1}: (8, {}), {2}: (9, {})} | custom-call | flops 167772160 | bytes 1048576 | tf_op jit(solution)/shard_map/chunk_whole/pallas_call | solution.py:348
  29.1 1.3 %collective-permute-done.9.refs_12_ = bf16[64,1024]{1,0:T(8,128)(2,1)S(1)} collective-permute-done((bf16[64,1024]{1,0:T(8,128)(2,1)S(1)}, bf16[64,1024]{1,0:T(8,128)(2,1)S(1)}, u32[]{:S(2)}, u32[]{:S(2)}) %collective-permute-start.9) | collective-permute-done | bytes 131104 | tf_op jit(solution)/shard_map/ppermute | solution.py:37
  30.4 1.7 %chunk_front.1 = (bf16[128,4096]{1,0:T(8,128)(2,1)}, bf16[64,1024]{1,0:T(8,128)(2,1)S(1)}, f32[64,128]{1,0:T(8,128)S(1)}, bf16[64,1024]{1,0:T(8,128)(2,1)S(1)}, ...) custom-call(bf16[128,4096]{1,0:T(8,128)(2,1)S(1)} %bitcast.18, ...), custom_call_target="tpu_custom_call", output_to_operand_aliasing={{0}: (7, {}), {1}: (8, {})} | custom-call | flops 167772160 | bytes 1048576 | tf_op jit(solution)/shard_map/chunk_front/pallas_call | solution.py:348
  32.1 1.1 %collective-permute-start.10 = (bf16[64,1024]{1,0:T(8,128)(2,1)S(1)}, bf16[64,1024]{1,0:T(8,128)(2,1)S(1)}, u32[]{:S(2)}, u32[]{:S(2)}) collective-permute-start(bf16[64,1024]{1,0:T(8,128)(2,1)S(1)} %get-tuple-element.71), channel_id=1, source_target_pairs={{0,12},{4,0},{8,4},{12,8},{1,13},{5,1},{9,5},{13,9},{2,14},{6,2},{... | collective-permute-start | bytes 393224 | tf_op jit(solution)/shard_map/ppermute | solution.py:37
  33.3 0.2 collective-permute-done.11.refs_10_
  33.4 0.6 %chunk_back.1 = (bf16[64,1024]{1,0:T(8,128)(2,1)S(1)}, bf16[128,512]{1,0:T(8,128)(2,1)S(1)}, bf16[16,1024]{1,0:T(8,128)(2,1)S(1)}, bf16[16,1024]{1,0:T(8,128)(2,...) custom-call(bf16[128,4096]{1,0:T(8,128)(2,1)S(1)} %bitcast.19, bf16[64,128]{1,0:T(8,128)(2,1)S(1)} %bitcast.33, ...), custom_call_target="tpu_custom_call" | custom-call | flops 167772160 | bytes 1048576 | tf_op jit(solution)/shard_map/chunk_back/pallas_call | solution.py:348
  34.1 1.6 %collective-permute-start.12 = (bf16[16,1024]{1,0:T(8,128)(2,1)S(1)}, bf16[16,1024]{1,0:T(8,128)(2,1)S(1)}, u32[]{:S(2)}, u32[]{:S(2)}) collective-permute-start(bf16[16,1024]{1,0:T(8,128)(2,1)S(1)} %get-tuple-element.87), channel_id=1, source_target_pairs={{0,1},{1,0},{2,3},{3,2},{4,5},{5,4},{6,7},{7,6},{8,9},{9,8},{10,11... | collective-permute-start | bytes 98312 | tf_op jit(solution)/shard_map/ppermute | solution.py:444
  35.7 2.6 %collective-permute-start.13 = (bf16[16,1024]{1,0:T(8,128)(2,1)S(1)}, bf16[16,1024]{1,0:T(8,128)(2,1)S(1)}, u32[]{:S(2)}, u32[]{:S(2)}) collective-permute-start(bf16[16,1024]{1,0:T(8,128)(2,1)S(1)} %get-tuple-element.88), channel_id=1, source_target_pairs={{0,2},{1,3},{2,0},{3,1},{4,6},{5,7},{6,4},{7,5},{8,10},{9,11},{10,... | collective-permute-start | bytes 98312 | tf_op jit(solution)/shard_map/ppermute | solution.py:444
  38.3 0.2 collective-permute-start.14
  38.5 1.6 %chunk_finish.1 = (bf16[128,4096]{1,0:T(8,128)(2,1)}, f32[128,1024]{1,0:T(8,128)S(1)}, bf16[64,128]{1,0:T(8,128)(2,1)}, bf16[128,1024]{1,0:T(8,128)(2,1)}) custom-call(bf16[128,4096]{1,0:T(8,128)(2,1)S(1)} %bitcast.20, bf16[64,128]{1,0:T(8,128)(2,1)S(1)} %bitcast.34, ...), custom_call_target="tpu_custom_call", output_to_operand_aliasing={{0}: (8, {}), {1}: (9, {})} | custom-call | flops 167772160 | bytes 1048576 | tf_op jit(solution)/shard_map/chunk_finish/pallas_call | solution.py:348
  40.1 0.7 %collective-permute-done.13 = bf16[16,1024]{1,0:T(8,128)(2,1)S(1)} collective-permute-done((bf16[16,1024]{1,0:T(8,128)(2,1)S(1)}, bf16[16,1024]{1,0:T(8,128)(2,1)S(1)}, u32[]{:S(2)}, u32[]{:S(2)}) %collective-permute-start.13) | collective-permute-done | bytes 32800 | tf_op jit(solution)/shard_map/ppermute | solution.py:444
  40.8 3.2 %collective-permute-done.14 = bf16[16,1024]{1,0:T(8,128)(2,1)S(1)} collective-permute-done((bf16[16,1024]{1,0:T(8,128)(2,1)S(1)}, bf16[16,1024]{1,0:T(8,128)(2,1)S(1)}, u32[]{:S(2)}, u32[]{:S(2)}) %collective-permute-start.14) | collective-permute-done | bytes 32800 | tf_op jit(solution)/shard_map/ppermute | solution.py:444
  44.0 0.6 %add_bitcast_fusion = f32[1,16,1024]{2,1,0:T(8,128)} fusion(bf16[16,1024]{1,0:T(8,128)(2,1)S(1)} %collective-permute-done.14, bf16[16,1024]{1,0:T(8,128)(2,1)S(1)} %collective-permute-done.13, bf16[16,1024]{1,0:T(8,128)(2,1)S(1)} %collective-permute-done.12, bf16[16,1024]{1,0:T(8,128)(2,1)S(1)} %get-tuple-element.86), kind=kLoop, calls=%fused_computation.1 | loop fusion | flops 114688 | bytes 196608 | tf_op jit(solution)/shard_map/broadcast_in_dim | solution.py:474
  (24 shorter events, 0.2 us)
Async XLA Ops:
  1.6 13.9 %copy-start = (bf16[1,1,128,4096]{3,2,1,0:T(8,128)(2,1)S(1)}, bf16[1,1,128,4096]{3,2,1,0:T(8,128)(2,1)}, u32[]{:S(2)}) copy-start(bf16[1,1,128,4096]{3,2,1,0:T(8,128)(2,1)} %param.6) | copy-start | bytes 3145732
  1.6 9.7 %collective-permute-start.7 = (bf16[128,1024]{1,0:T(8,128)(2,1)S(1)}, bf16[128,1024]{1,0:T(8,128)(2,1)S(1)}, u32[]{:S(2)}, u32[]{:S(2)}) collective-permute-start(bf16[128,1024]{1,0:T(8,128)(2,1)S(1)} %split_columns.2.rest_0_), channel_id=1, source_target_pairs={{0,16},{16,0},{1,17},{17,1},{2,18},{18,2},{3,19},{19,3},{4,20},{20... | collective-permute-start | bytes 786440 | tf_op jit(solution)/shard_map/ppermute | solution.py:37
  4.6 6.2 %copy-start.5 = (s32[1,1,512]{2,1,0:T(1,128)S(1)}, s32[1,1,512]{2,1,0:T(1,128)}, u32[]{:S(2)}) copy-start(s32[1,1,512]{2,1,0:T(1,128)} %param.11) | copy-start | bytes 6148
  6.6 0.7 %copy-start.3 = (bf16[64,1024]{1,0:T(8,128)(2,1)}, bf16[64,1024]{1,0:T(8,128)(2,1)S(1)}, u32[]{:S(2)}) copy-start(bf16[64,1024]{1,0:T(8,128)(2,1)S(1)} %get-tuple-element.50) | copy-start | bytes 393220
  7.3 8.2 %copy-start.1 = (bf16[1,1,128,1024]{3,2,1,0:T(8,128)(2,1)S(1)}, bf16[1,1,128,1024]{3,2,1,0:T(8,128)(2,1)}, u32[]{:S(2)}) copy-start(bf16[1,1,128,1024]{3,2,1,0:T(8,128)(2,1)} %param.7) | copy-start | bytes 786436
  7.3 9.6 %collective-permute-start.5 = (bf16[64,1024]{1,0:T(8,128)(2,1)S(1)}, bf16[64,1024]{1,0:T(8,128)(2,1)S(1)}, u32[]{:S(2)}, u32[]{:S(2)}) collective-permute-start(bf16[64,1024]{1,0:T(8,128)(2,1)S(1)} %get-tuple-element.48.refs_5_), channel_id=1, source_target_pairs={{0,8},{4,12},{8,0},{12,4},{1,9},{5,13},{9,1},{13,5},{2,10},{6,14},... | collective-permute-start | bytes 393224 | tf_op jit(solution)/shard_map/ppermute | solution.py:37
  8.8 6.7 %collective-permute-start = (bf16[128,1024]{1,0:T(8,128)(2,1)}, bf16[128,1024]{1,0:T(8,128)(2,1)S(1)}, u32[]{:S(2)}, u32[]{:S(2)}) collective-permute-start(bf16[128,1024]{1,0:T(8,128)(2,1)} %get-tuple-element.47), channel_id=1, source_target_pairs={{0,4},{4,8},{8,12},{12,0},{1,5},{5,9},{9,13},{13,1},{2,6},{6,10},{... | collective-permute-start | bytes 786440 | tf_op jit(solution)/shard_map/ppermute | solution.py:37
  8.8 18.5 %collective-permute-start.4 = (bf16[128,1024]{1,0:T(8,128)(2,1)S(1)}, bf16[128,1024]{1,0:T(8,128)(2,1)S(1)}, u32[]{:S(2)}, u32[]{:S(2)}) collective-permute-start(bf16[128,1024]{1,0:T(8,128)(2,1)S(1)} %get-tuple-element.51), channel_id=1, source_target_pairs={{0,16},{16,0},{1,17},{17,1},{2,18},{18,2},{3,19},{19,3},{4,20},{20... | collective-permute-start | bytes 786440 | tf_op jit(solution)/shard_map/ppermute | solution.py:37
  9.4 14.2 %collective-permute-start.6 = (bf16[128,1024]{1,0:T(8,128)(2,1)S(1)}, bf16[128,1024]{1,0:T(8,128)(2,1)S(1)}, u32[]{:S(2)}, u32[]{:S(2)}) collective-permute-start(bf16[128,1024]{1,0:T(8,128)(2,1)S(1)} %get-tuple-element.52), channel_id=1, source_target_pairs={{0,16},{16,0},{1,17},{17,1},{2,18},{18,2},{3,19},{19,3},{4,20},{20... | collective-permute-start | bytes 786440 | tf_op jit(solution)/shard_map/ppermute | solution.py:37
  11.2 4.3 %copy-start.2 = (bf16[1,1,128,64]{2,3,1,0:T(8,128)(2,1)S(1)}, bf16[1,1,128,64]{2,3,1,0:T(8,128)(2,1)}, u32[]{:S(2)}) copy-start(bf16[1,1,128,64]{2,3,1,0:T(8,128)(2,1)} %param.8) | copy-start | bytes 49156
  11.3 14.1 %collective-permute-start.3 = (bf16[64,1024]{1,0:T(8,128)(2,1)S(1)}, bf16[64,1024]{1,0:T(8,128)(2,1)S(1)}, u32[]{:S(2)}, u32[]{:S(2)}) collective-permute-start(bf16[64,1024]{1,0:T(8,128)(2,1)S(1)} %get-tuple-element.48.refs_5_), channel_id=1, source_target_pairs={{0,12},{4,0},{8,4},{12,8},{1,13},{5,1},{9,5},{13,9},{2,14},{6,2},{... | collective-permute-start | bytes 393224 | tf_op jit(solution)/shard_map/ppermute | solution.py:37
  15.5 1.4 %copy-start.4 = (bf16[64,1024]{1,0:T(8,128)(2,1)S(1)}, bf16[64,1024]{1,0:T(8,128)(2,1)}, u32[]{:S(2)}) copy-start(bf16[64,1024]{1,0:T(8,128)(2,1)} %copy-done.3) | copy-start | bytes 393220
  16.8 10.6 %collective-permute-start.8 = (bf16[64,1024]{1,0:T(8,128)(2,1)S(1)}, bf16[64,1024]{1,0:T(8,128)(2,1)S(1)}, u32[]{:S(2)}, u32[]{:S(2)}) collective-permute-start(bf16[64,1024]{1,0:T(8,128)(2,1)S(1)} %get-tuple-element.64), channel_id=1, source_target_pairs={{0,12},{4,0},{8,4},{12,8},{1,13},{5,1},{9,5},{13,9},{2,14},{6,2},{... | collective-permute-start | bytes 393224 | tf_op jit(solution)/shard_map/ppermute | solution.py:37
  16.9 12.2 %collective-permute-start.2 = (bf16[64,1024]{1,0:T(8,128)(2,1)S(1)}, bf16[64,1024]{1,0:T(8,128)(2,1)S(1)}, u32[]{:S(2)}, u32[]{:S(2)}) collective-permute-start(bf16[64,1024]{1,0:T(8,128)(2,1)S(1)} %copy-done.4), channel_id=1, source_target_pairs={{0,16},{16,0},{1,17},{17,1},{2,18},{18,2},{3,19},{19,3},{4,20},{20... | collective-permute-start | bytes 393224 | tf_op jit(solution)/shard_map/ppermute | solution.py:37
  25.4 5.1 %collective-permute-start.9 = (bf16[64,1024]{1,0:T(8,128)(2,1)S(1)}, bf16[64,1024]{1,0:T(8,128)(2,1)S(1)}, u32[]{:S(2)}, u32[]{:S(2)}) collective-permute-start(bf16[64,1024]{1,0:T(8,128)(2,1)S(1)} %get-tuple-element.70), channel_id=1, source_target_pairs={{0,8},{4,12},{8,0},{12,4},{1,9},{5,13},{9,1},{13,5},{2,10},{6,14},... | collective-permute-start | bytes 393224 | tf_op jit(solution)/shard_map/ppermute | solution.py:37
  25.4 7.8 %collective-permute-start.1 = (bf16[64,1024]{1,0:T(8,128)(2,1)S(1)}, bf16[64,1024]{1,0:T(8,128)(2,1)S(1)}, u32[]{:S(2)}, u32[]{:S(2)}) collective-permute-start(bf16[64,1024]{1,0:T(8,128)(2,1)S(1)} %get-tuple-element.49), channel_id=1, source_target_pairs={{0,16},{16,0},{1,17},{17,1},{2,18},{18,2},{3,19},{19,3},{4,20},{20... | collective-permute-start | bytes 393224 | tf_op jit(solution)/shard_map/ppermute | solution.py:37
  29.0 4.4 %collective-permute-start.11 = (bf16[64,1024]{1,0:T(8,128)(2,1)S(1)}, bf16[64,1024]{1,0:T(8,128)(2,1)S(1)}, u32[]{:S(2)}, u32[]{:S(2)}) collective-permute-start(bf16[64,1024]{1,0:T(8,128)(2,1)S(1)} %get-tuple-element.79), channel_id=1, source_target_pairs={{0,4},{4,8},{8,12},{12,0},{1,5},{5,9},{9,13},{13,1},{2,6},{6,10},{... | collective-permute-start | bytes 393224 | tf_op jit(solution)/shard_map/ppermute | solution.py:37
  32.1 6.4 %collective-permute-start.10 = (bf16[64,1024]{1,0:T(8,128)(2,1)S(1)}, bf16[64,1024]{1,0:T(8,128)(2,1)S(1)}, u32[]{:S(2)}, u32[]{:S(2)}) collective-permute-start(bf16[64,1024]{1,0:T(8,128)(2,1)S(1)} %get-tuple-element.71), channel_id=1, source_target_pairs={{0,12},{4,0},{8,4},{12,8},{1,13},{5,1},{9,5},{13,9},{2,14},{6,2},{... | collective-permute-start | bytes 393224 | tf_op jit(solution)/shard_map/ppermute | solution.py:37
  34.1 6.0 %collective-permute-start.12 = (bf16[16,1024]{1,0:T(8,128)(2,1)S(1)}, bf16[16,1024]{1,0:T(8,128)(2,1)S(1)}, u32[]{:S(2)}, u32[]{:S(2)}) collective-permute-start(bf16[16,1024]{1,0:T(8,128)(2,1)S(1)} %get-tuple-element.87), channel_id=1, source_target_pairs={{0,1},{1,0},{2,3},{3,2},{4,5},{5,4},{6,7},{7,6},{8,9},{9,8},{10,11... | collective-permute-start | bytes 98312 | tf_op jit(solution)/shard_map/ppermute | solution.py:444
  35.7 5.1 %collective-permute-start.13 = (bf16[16,1024]{1,0:T(8,128)(2,1)S(1)}, bf16[16,1024]{1,0:T(8,128)(2,1)S(1)}, u32[]{:S(2)}, u32[]{:S(2)}) collective-permute-start(bf16[16,1024]{1,0:T(8,128)(2,1)S(1)} %get-tuple-element.88), channel_id=1, source_target_pairs={{0,2},{1,3},{2,0},{3,1},{4,6},{5,7},{6,4},{7,5},{8,10},{9,11},{10,... | collective-permute-start | bytes 98312 | tf_op jit(solution)/shard_map/ppermute | solution.py:444
  38.3 5.7 %collective-permute-start.14 = (bf16[16,1024]{1,0:T(8,128)(2,1)S(1)}, bf16[16,1024]{1,0:T(8,128)(2,1)S(1)}, u32[]{:S(2)}, u32[]{:S(2)}) collective-permute-start(bf16[16,1024]{1,0:T(8,128)(2,1)S(1)} %get-tuple-element.89), channel_id=1, source_target_pairs={{0,3},{1,2},{2,1},{3,0},{4,7},{5,6},{6,5},{7,4},{8,11},{9,10},{10,... | collective-permute-start | bytes 98312 | tf_op jit(solution)/shard_map/ppermute | solution.py:444
where the time goes:
time: 44.8 us; the launch traced here: 44.7 us
  starting transfers between devices  15.6 us (35%)
  waiting for transfers between devices  15 us (33%)
  Pallas kernels  11.6 us (26%)
  other arithmetic  0.92 us (2%)
  between operations  0.84 us (2%)
  local copies, waits for them, and re-layouts  0.83 us (2%)
    ppermute x12, starting transfers between devices, passed_along(): return lax.ppermute(value, axis, pairs)  11.1 us
    ppermute x12, waiting for transfers between devices, passed_along(): return lax.ppermute(value, axis, pairs)  11.1 us
    pallas_call x6, Pallas kernels, chunk_step(): pl.pallas_call(functools.partial(chunk_kernel, step, phase, chunks, up_ro...  8.58 us
    ppermute x3, starting transfers between devices, per_device(): lax.ppermute(getattr(carried, SHARES[away]), 'dp', pairs)  4.45 us
    ppermute x3, waiting for transfers between devices, per_device(): lax.ppermute(getattr(carried, SHARES[away]), 'dp', pairs)  3.91 us
    pallas_call x2, Pallas kernels, split_columns(): pl.pallas_call(functools.partial(split_kernel, steps, chunks, bundled), i...  2.98 us
  transfers between devices with their start and end apart: 15, of which 6 were waited for; matrix products, arithmetic and copies ran while one was open for 1% of the time, Pallas kernels for 24%

commit v1 on v0

--- a/solution.py
+++ b/solution.py
@@ -21,6 +21,7 @@
 IN = "_in"
 DQ = "dq_out"
 DQ_IN = DQ + IN
+UPSTREAM = "upstream"
 SHARES = ["share" + str(index) for index in range(64)]
 PENDING = ["pending" + str(index) for index in range(2)]
 TERMS = ["term_in" + str(index) for index in range(64)]
@@ -37,12 +38,6 @@
     return lax.ppermute(value, axis, pairs)
 
 
-def partner(place, away, count):
-    if count & (count - 1) == 0:
-        return place ^ away
-    return (place + away) % count
-
-
 def dot(left, right, left_dim, right_dim):
     return lax.dot_general(
         left, right, (((left_dim,), (right_dim,)), ((), ())), preferred_element_type=jnp.float32
@@ -53,47 +48,46 @@
     return lax.rem(lax.axis_index("seq") + (2 * chunks - 1 - step), chunks)
 
 
-def split_kernel(steps, chunks, bundled, upstream, own, matrix, *rest):
+def piece_of(upstream, piece, chunks):
+    rows = upstream.shape[0]
+    width = upstream.shape[1] // chunks
+    step = min(piece, chunks - 1)
+    columns = pl.ds(pl.multiple_of(chunk_at(step, chunks) * width, HEAD_SIZE), width)
+    if piece < chunks - 1:
+        return upstream.at[:, columns]
+    return upstream.at[pl.ds((piece - step) * (rows // BLOCKS), rows // BLOCKS), columns]
+
+
+def piece_shape(upstream, piece, chunks):
+    rows = upstream.shape[0] if piece < chunks - 1 else upstream.shape[0] // BLOCKS
+    return jax.ShapeDtypeStruct((rows, upstream.shape[1] // chunks), upstream.dtype)
+
+
+def split_kernel(piece, chunks, bundled, upstream, own, matrix, *rest):
     rest = list(rest)
     sems = rest.pop()
-    if steps[0] > 0:
+    if piece > 0:
         rest.pop(0)
-    rows = upstream.shape[0]
-    width = upstream.shape[1] // chunks
     copies = []
 
     def send(source, target):
         copies.append(pltpu.make_async_copy(source, target, sems.at[len(copies)]))
         copies[-1].start()
 
-    for step in steps:
-        start = pl.multiple_of(chunk_at(step, chunks) * width, HEAD_SIZE)
-        columns = pl.ds(start, width)
-        if step < chunks - 1:
-            send(upstream.at[:, columns], rest.pop(0))
-        else:
-            send(upstream.at[pl.ds(0, rows // BLOCKS), columns], rest.pop(0))
-            send(upstream.at[pl.ds(rows // BLOCKS, rows // BLOCKS), columns], rest.pop(0))
-    if steps[0] > 0:
+    send(piece_of(upstream, piece, chunks), rest.pop(0))
+    if piece == 2:
         send(matrix, rest.pop(0))
     if bundled > 0:
         bundle = rest.pop(0)
-        send(own.at[pl.ds(rows - bundled, bundled)], bundle.at[pl.ds(0, bundled)])
+        send(own.at[pl.ds(own.shape[0] - bundled, bundled)], bundle.at[pl.ds(0, bundled)])
         send(matrix, bundle.at[pl.ds(bundled, matrix.shape[0])])
     for copy in copies:
         copy.wait()
 
 
-def split_columns(steps, chunks, bundled, upstream, own, matrix, after):
-    rows, columns = upstream.shape
-    shapes = []
-    for step in steps:
-        if step < chunks - 1:
-            shapes.append(jax.ShapeDtypeStruct((rows, columns // chunks), upstream.dtype))
-        else:
-            half = jax.ShapeDtypeStruct((rows // BLOCKS, columns // chunks), upstream.dtype)
-            shapes += [half] * BLOCKS
-    if steps[0] > 0:
+def split_piece(piece, chunks, bundled, upstream, own, matrix, after):
+    shapes = [piece_shape(upstream, piece, chunks)]
+    if piece == 2:
         shapes.append(jax.ShapeDtypeStruct(matrix.shape, matrix.dtype))
     if bundled > 0:
         shapes.append(jax.ShapeDtypeStruct((bundled + matrix.shape[0], own.shape[1]), own.dtype))
@@ -102,16 +96,16 @@
     ] + after
     return list(
         pl.pallas_call(
-            functools.partial(split_kernel, steps, chunks, bundled),
+            functools.partial(split_kernel, piece, chunks, bundled),
             in_specs=[HBM] * 3 + [VMEM] * len(after),
             out_specs=[VMEM] * len(shapes),
             out_shape=shapes,
             scratch_shapes=[pltpu.SemaphoreType.DMA((len(shapes) + 1,))],
             compiler_params=pltpu.CompilerParams(vmem_limit_bytes=LIMIT),
             cost_estimate=pl.CostEstimate(
-                flops=0, bytes_accessed=4 * rows * columns, transcendentals=0
+                flops=0, bytes_accessed=4 * upstream.size // chunks, transcendentals=0
             ),
-            name="split_columns",
+            name="split_piece",
         )(*operands)
     )
 
@@ -172,6 +166,10 @@
         return pl.ds(pl.multiple_of(chunk_at(at_step, chunks) * width, HEAD_SIZE), width)
 
     copies = []
+    if hasattr(refs, "piece_out"):
+        piece = piece_of(refs.upstream, step + 3, chunks)
+        copies.append(pltpu.make_async_copy(piece, refs.piece_out, refs.sems.at[2]))
+        copies[-1].start()
     for index, (at_step, start, count) in enumerate(pending):
         target = refs.dq_out.at[pl.ds(start, count), columns_of(at_step)]
         copies.append(pltpu.make_async_copy(getattr(refs, PENDING[index]), target, refs.sems.at[index]))
@@ -244,7 +242,7 @@
         shares = [name for name in names if name in SHARES]
         share_rows = rank // len(shares)
         for away, name in enumerate(shares):
-            target = partner(lax.axis_index("dp"), away, len(shares))
+            target = lax.rem(lax.axis_index("dp") + away, len(shares))
             start = pl.multiple_of(target * share_rows, share_rows)
             getattr(refs, name)[...] = total[pl.ds(start, share_rows)]
 
@@ -319,6 +317,10 @@
             outputs[SHARES[away]] = ((rank // packs, width), jnp.bfloat16)
 
     operands = dict(vars(inputs))
+    if phase != WHOLE or step + 3 > chunks:
+        del operands[UPSTREAM]
+    else:
+        outputs.update(piece_out=None)
     if hasattr(inputs, "halo_back"):
         outputs.update(pair_out=((rows, chunks * PAIR), jnp.bfloat16))
     aliases = {}
@@ -339,17 +341,20 @@
         operands[PENDING[index]] = array
     for index, term in enumerate(terms):
         operands[TERMS[index]] = term
+    shapes = [shape and jax.ShapeDtypeStruct(*shape) for shape in outputs.values()]
+    if hasattr(inputs, UPSTREAM) and None in shapes:
+        shapes[shapes.index(None)] = piece_shape(inputs.upstream, step + 3, chunks)
     scratch = dict(
         total=pltpu.VMEM((rank, width), jnp.bfloat16),
-        sems=pltpu.SemaphoreType.DMA((2,)),
+        sems=pltpu.SemaphoreType.DMA((3,)),
     )
     names = list(operands) + list(outputs) + list(scratch)
     places = [(at_step, start, array.shape[0]) for at_step, start, array in pending]
     results = pl.pallas_call(
         functools.partial(chunk_kernel, step, phase, chunks, up_row, places, names),
-        in_specs=[HBM if name == DQ_IN else VMEM for name in operands],
+        in_specs=[HBM if name in (DQ_IN, UPSTREAM) else VMEM for name in operands],
         out_specs=[HBM if name == DQ else VMEM for name in outputs],
-        out_shape=[jax.ShapeDtypeStruct(*shape) for shape in outputs.values()],
+        out_shape=shapes,
         scratch_shapes=list(scratch.values()),
         input_output_aliases=aliases,
         compiler_params=pltpu.CompilerParams(vmem_limit_bytes=LIMIT),
@@ -386,10 +391,14 @@
     own_matrix = adapter_up_matrix[0]
     bundled = span if len(pieces) == 1 and own_matrix.shape[1] == own.shape[1] else 0
 
-    parts = split_columns(steps[:1], chunks, 0, upstream[0, 0], own, own_matrix, [])
-    parts += split_columns(steps[1:], chunks, bundled, upstream[0, 0], own, own_matrix, parts[:1])
-    cots = [passed_along(part, "section", -1) for part in parts[: chunks + 1]]
-    own_matrix = parts[chunks + 1]
+    cotangents = upstream[0, 0]
+    sources = (cotangents, own, own_matrix)
+    first_piece = split_piece(0, chunks, 0, *sources, [])
+    cots = [passed_along(first_piece[0], "section", -1)]
+    parts = split_piece(1, chunks, bundled, *sources, first_piece)
+    cots.append(passed_along(parts[0], "section", -1))
+    later_part, own_matrix = split_piece(2, chunks, 0, *sources, cots[:1])
+    cots.append(passed_along(later_part, "section", -1))
     if bundled > 0:
         halo = passed_along(parts[-1], "seq", 1)
         matrices, up_rows = [halo], [span]
@@ -416,7 +425,12 @@
     bias = jnp.concatenate([bias, bias], axis=1)
 
     inputs = SimpleNamespace(
-        fq=frozen_queries[0, 0], at=adapter_input[0, 0].T, halo=halo, own=own, bias=bias
+        fq=frozen_queries[0, 0],
+        at=adapter_input[0, 0].T,
+        halo=halo,
+        own=own,
+        bias=bias,
+        upstream=pltpu.with_memory_space_constraint(cotangents, pltpu.HBM),
     )
     carried, terms, pending = SimpleNamespace(), [], []
     for step in steps:
@@ -434,14 +448,16 @@
                 pending.append((step, block, carried.grad_out))
             else:
                 pending = [(step, 0, carried.grad_out)]
+            if phase == WHOLE and step + 3 <= chunks:
+                cots.append(passed_along(carried.piece_out, "section", -1))
             if phase == WHOLE:
                 terms.append(passed_along(carried.term_out, "seq", -(step + 1)))
 
     packs = lax.axis_size("dp")
     weight_share = carried.share0.astype(jnp.float32)
     for away in range(1, packs):
-        pairs = [(source, partner(source, away, packs)) for source in range(packs)]
-        weight_share += lax.ppermute(getattr(carried, SHARES[away]), "dp", pairs).astype(jnp.float32)
+        share = passed_along(getattr(carried, SHARES[away]), "dp", away)
+        weight_share += share.astype(jnp.float32)
 
     halo_grads = carried.halo_out
     if per_head > 1:

time: 44.8 us -> 40.8 us (0.911)
  waiting for transfers between devices: 15 us -> 7.13 us
  starting transfers between devices: 15.6 us -> 18.1 us
  Pallas kernels: 11.6 us -> 12.7 us
    ppermute x12 -> x15, starting transfers between devices: 11.1 us -> 18.1 us  [passed_along(): return lax.ppermute(value, axis, pairs)]
    ppermute x3 -> x0, starting transfers between devices: 4.45 us -> none  [per_device(): lax.ppermute(getattr(carried, SHARES[away]), 'dp', pairs)]
    ppermute x12 -> x15, waiting for transfers between devices: 11.1 us -> 7.13 us  [passed_along(): return lax.ppermute(value, axis, pairs)]
    ppermute x3 -> x0, waiting for transfers between devices: 3.91 us -> none  [per_device(): lax.ppermute(getattr(carried, SHARES[away]), 'dp', pairs)]
    pallas_call x6, Pallas kernels: 8.58 us -> 9.68 us  [chunk_step(): pl.pallas_call(functools.partial(chunk_kernel, step, phase, chunks, up_ro...]
    pallas_call x2 -> x3, Pallas kernels: 2.98 us -> 3.07 us  [split_piece(): pl.pallas_call(functools.partial(split_kernel, piece, chunks, bundled), i...]
  transfers between devices with their start and end apart: 15 -> 15, of which waited for: 6 -> 4; matrix products, arithmetic and copies ran while one was open for 1% -> 1% of each run, Pallas kernels for 24% -> 29%
where the time goes in v1:
time: 40.8 us; the launch traced here: 40.6 us
  starting transfers between devices  18.1 us (44%)
  Pallas kernels  12.7 us (31%)
  waiting for transfers between devices  7.13 us (17%)
  other arithmetic  0.92 us (2%)
  local copies, waits for them, and re-layouts  0.84 us (2%)
  between operations  0.82 us (2%)
    ppermute x15, starting transfers between devices, passed_along(): return lax.ppermute(value, axis, pairs)  18.1 us
    pallas_call x6, Pallas kernels, chunk_step(): pl.pallas_call(functools.partial(chunk_kernel, step, phase, chunks, up_ro...  9.68 us
    ppermute x15, waiting for transfers between devices, passed_along(): return lax.ppermute(value, axis, pairs)  7.13 us
    pallas_call x3, Pallas kernels, split_piece(): pl.pallas_call(functools.partial(split_kernel, piece, chunks, bundled), i...  3.07 us
  transfers between devices with their start and end apart: 15, of which 4 were waited for; matrix products, arithmetic and copies ran while one was open for 1% of the time, Pallas kernels for 29%

profile of v1, /device:TPU:0, one launch (start us, length us, event | category | flops | bytes accessed | tf_op | source)
XLA Modules:
  0.0 40.6 jit_solution(2482532381097245453)
XLA Ops:
  0.6 1.0 %split_piece.3.rest_0_ = bf16[128,1024]{1,0:T(8,128)(2,1)S(1)} custom-call(bf16[128,4096]{1,0:T(8,128)(2,1)} %bitcast.36, bf16[128,1024]{1,0:T(8,128)(2,1)} %bitcast.21, bf16[64,1024]{1,0:T(8,128)(2,1)} %bitcast.42), custom_call_target="tpu_custom_call" | custom-call | bytes 524288 | tf_op jit(solution)/shard_map/split_piece/pallas_call | solution.py:98
  1.6 3.0 %collective-permute-start.1 = (bf16[128,1024]{1,0:T(8,128)(2,1)S(1)}, bf16[128,1024]{1,0:T(8,128)(2,1)S(1)}, u32[]{:S(2)}, u32[]{:S(2)}) collective-permute-start(bf16[128,1024]{1,0:T(8,128)(2,1)S(1)} %split_piece.3.rest_0_), channel_id=1, source_target_pairs={{0,16},{16,0},{1,17},{17,1},{2,18},{18,2},{3,19},{19,3},{4,20},{20... | collective-permute-start | bytes 786440 | tf_op jit(solution)/shard_map/ppermute | solution.py:38
  4.6 1.1 %split_piece.4 = (bf16[128,1024]{1,0:T(8,128)(2,1)S(1)}, bf16[128,1024]{1,0:T(8,128)(2,1)S(1)}) custom-call(bf16[128,4096]{1,0:T(8,128)(2,1)} %bitcast.37, bf16[128,1024]{1,0:T(8,128)(2,1)} %bitcast.22, bf16[64,1024]{1,0:T(8,128)(2,1)} %bitcast.43, bf16[128,1024]{1,0:T(8,128)(2,1)S(1)} %split_piece.3.rest_0_), custom_call_target="tpu_custom_call" | custom-call | bytes 524288 | tf_op jit(solution)/shard_map/split_piece/pallas_call | solution.py:98
  5.8 0.1 collective-permute-start.3
  5.9 0.7 %copy-done.3 = s32[1,1,512]{2,1,0:T(1,128)S(1)} copy-done((s32[1,1,512]{2,1,0:T(1,128)S(1)}, s32[1,1,512]{2,1,0:T(1,128)}, u32[]{:S(2)}) %copy-start.3) | copy-done | bytes 2072
  6.5 0.1 pad_dynamic-slice_fusion
  6.6 0.1 fusion.5
  6.7 0.1 fusion.4
  6.8 0.1 fusion.2
  6.9 4.9 %collective-permute-done.1.rest_0_.refs_7_ = bf16[128,1024]{1,0:T(8,128)(2,1)S(1)} collective-permute-done((bf16[128,1024]{1,0:T(8,128)(2,1)S(1)}, bf16[128,1024]{1,0:T(8,128)(2,1)S(1)}, u32[]{:S(2)}, u32[]{:S(2)}) %collective-permute-start.1) | collective-permute-done | bytes 262176 | tf_op jit(solution)/shard_map/ppermute | solution.py:38
  11.8 1.0 %split_piece.5 = (bf16[128,1024]{1,0:T(8,128)(2,1)S(1)}, bf16[64,1024]{1,0:T(8,128)(2,1)S(1)}) custom-call(bf16[128,4096]{1,0:T(8,128)(2,1)} %bitcast.38, bf16[128,1024]{1,0:T(8,128)(2,1)} %bitcast.23, bf16[64,1024]{1,0:T(8,128)(2,1)} %bitcast.44, bf16[128,1024]{1,0:T(8,128)(2,1)S(1)} %collective-permute-done.1.rest_0_.refs_7_), custom_call_target="tpu_custom_call" | custom-call | bytes 524288 | tf_op jit(solution)/shard_map/split_piece/pallas_call | solution.py:98
  12.8 2.2 %collective-permute-start.2 = (bf16[64,1024]{1,0:T(8,128)(2,1)S(1)}, bf16[64,1024]{1,0:T(8,128)(2,1)S(1)}, u32[]{:S(2)}, u32[]{:S(2)}) collective-permute-start(bf16[64,1024]{1,0:T(8,128)(2,1)S(1)} %get-tuple-element.48.refs_5_), channel_id=1, source_target_pairs={{0,8},{4,12},{8,0},{12,4},{1,9},{5,13},{9,1},{13,5},{2,10},{6,14},... | collective-permute-start | bytes 393224 | tf_op jit(solution)/shard_map/ppermute | solution.py:38
  14.9 1.5 %collective-permute-start.7 = (bf16[128,1024]{1,0:T(8,128)(2,1)S(1)}, bf16[128,1024]{1,0:T(8,128)(2,1)S(1)}, u32[]{:S(2)}, u32[]{:S(2)}) collective-permute-start(bf16[128,1024]{1,0:T(8,128)(2,1)S(1)} %get-tuple-element.57), channel_id=1, source_target_pairs={{0,16},{16,0},{1,17},{17,1},{2,18},{18,2},{3,19},{19,3},{4,20},{20... | collective-permute-start | bytes 786440 | tf_op jit(solution)/shard_map/ppermute | solution.py:38
  16.4 0.1 maximum_maximum_fusion.refs_4_
  16.7 2.1 %chunk_whole.3 = (bf16[64,1024]{1,0:T(8,128)(2,1)S(1)}, f32[128,1024]{1,0:T(8,128)S(1)}, f32[64,128]{1,0:T(8,128)S(1)}, bf16[128,1024]{1,0:T(8,128)(2,1)S(1)}, b...) custom-call(bf16[128,4096]{1,0:T(8,128)(2,1)S(1)} %bitcast.15, ...), custom_call_target="tpu_custom_call" | custom-call | flops 167772160 | bytes 1048576 | tf_op jit(solution)/shard_map/chunk_whole/pallas_call | solution.py:353
  18.8 0.6 %collective-permute-start.8 = (bf16[64,1024]{1,0:T(8,128)(2,1)S(1)}, bf16[64,1024]{1,0:T(8,128)(2,1)S(1)}, u32[]{:S(2)}, u32[]{:S(2)}) collective-permute-start(bf16[64,1024]{1,0:T(8,128)(2,1)S(1)} %get-tuple-element.64), channel_id=1, source_target_pairs={{0,12},{4,0},{8,4},{12,8},{1,13},{5,1},{9,5},{13,9},{2,14},{6,2},{... | collective-permute-start | bytes 393224 | tf_op jit(solution)/shard_map/ppermute | solution.py:38
  19.4 0.1 collective-permute-start.5
  19.5 2.0 %chunk_whole.4 = (bf16[128,4096]{1,0:T(8,128)(2,1)}, bf16[64,1024]{1,0:T(8,128)(2,1)S(1)}, f32[128,1024]{1,0:T(8,128)S(1)}, f32[64,128]{1,0:T(8,128)S(1)}, bf16[...) custom-call(bf16[128,4096]{1,0:T(8,128)(2,1)S(1)} %bitcast.16, ...), custom_call_target="tpu_custom_call", output_to_operand_aliasing={{1}: (8, {}), {2}: (9, {})} | custom-call | flops 167772160 | bytes 1048576 | tf_op jit(solution)/shard_map/chunk_whole/pallas_call | solution.py:353
  21.6 2.0 %collective-permute-start.9 = (bf16[64,1024]{1,0:T(8,128)(2,1)S(1)}, bf16[64,1024]{1,0:T(8,128)(2,1)S(1)}, u32[]{:S(2)}, u32[]{:S(2)}) collective-permute-start(bf16[64,1024]{1,0:T(8,128)(2,1)S(1)} %get-tuple-element.70), channel_id=1, source_target_pairs={{0,8},{4,12},{8,0},{12,4},{1,9},{5,13},{9,1},{13,5},{2,10},{6,14},... | collective-permute-start | bytes 393224 | tf_op jit(solution)/shard_map/ppermute | solution.py:38
  23.6 1.5 %collective-permute-start.4 = (bf16[64,1024]{1,0:T(8,128)(2,1)S(1)}, bf16[64,1024]{1,0:T(8,128)(2,1)S(1)}, u32[]{:S(2)}, u32[]{:S(2)}) collective-permute-start(bf16[64,1024]{1,0:T(8,128)(2,1)S(1)} %get-tuple-element.55), channel_id=1, source_target_pairs={{0,16},{16,0},{1,17},{17,1},{2,18},{18,2},{3,19},{19,3},{4,20},{20... | collective-permute-start | bytes 393224 | tf_op jit(solution)/shard_map/ppermute | solution.py:38
  25.1 1.6 %chunk_whole.5 = (bf16[128,4096]{1,0:T(8,128)(2,1)}, bf16[64,1024]{1,0:T(8,128)(2,1)S(1)}, f32[128,1024]{1,0:T(8,128)S(1)}, f32[64,128]{1,0:T(8,128)S(1)}, bf16[...) custom-call(bf16[128,4096]{1,0:T(8,128)(2,1)S(1)} %bitcast.17, ...), custom_call_target="tpu_custom_call", output_to_operand_aliasing={{0}: (7, {}), {1}: (8, {}), {2}: (9, {})} | custom-call | flops 167772160 | bytes 1048576 | tf_op jit(solution)/shard_map/chunk_whole/pallas_call | solution.py:353
  26.8 0.4 collective-permute-done.9.refs_12_
  27.2 1.7 %chunk_front.1 = (bf16[128,4096]{1,0:T(8,128)(2,1)}, bf16[64,1024]{1,0:T(8,128)(2,1)S(1)}, f32[64,128]{1,0:T(8,128)S(1)}, bf16[64,1024]{1,0:T(8,128)(2,1)S(1)}, ...) custom-call(bf16[128,4096]{1,0:T(8,128)(2,1)S(1)} %bitcast.18, ...), custom_call_target="tpu_custom_call", output_to_operand_aliasing={{0}: (7, {}), {1}: (8, {})} | custom-call | flops 167772160 | bytes 1048576 | tf_op jit(solution)/shard_map/chunk_front/pallas_call | solution.py:353
  28.9 1.4 %collective-permute-start.10 = (bf16[64,1024]{1,0:T(8,128)(2,1)S(1)}, bf16[64,1024]{1,0:T(8,128)(2,1)S(1)}, u32[]{:S(2)}, u32[]{:S(2)}) collective-permute-start(bf16[64,1024]{1,0:T(8,128)(2,1)S(1)} %get-tuple-element.71), channel_id=1, source_target_pairs={{0,12},{4,0},{8,4},{12,8},{1,13},{5,1},{9,5},{13,9},{2,14},{6,2},{... | collective-permute-start | bytes 393224 | tf_op jit(solution)/shard_map/ppermute | solution.py:38
  30.3 0.9 %collective-permute-done.11.refs_10_ = bf16[64,1024]{1,0:T(8,128)(2,1)S(1)} collective-permute-done((bf16[64,1024]{1,0:T(8,128)(2,1)S(1)}, bf16[64,1024]{1,0:T(8,128)(2,1)S(1)}, u32[]{:S(2)}, u32[]{:S(2)}) %collective-permute-start.11) | collective-permute-done | bytes 131104 | tf_op jit(solution)/shard_map/ppermute | solution.py:38
  31.2 0.6 %chunk_back.1 = (bf16[64,1024]{1,0:T(8,128)(2,1)S(1)}, bf16[128,512]{1,0:T(8,128)(2,1)S(1)}, bf16[16,1024]{1,0:T(8,128)(2,1)S(1)}, bf16[16,1024]{1,0:T(8,128)(2,...) custom-call(bf16[128,4096]{1,0:T(8,128)(2,1)S(1)} %bitcast.19, bf16[64,128]{1,0:T(8,128)(2,1)S(1)} %bitcast.34, ...), custom_call_target="tpu_custom_call" | custom-call | flops 167772160 | bytes 1048576 | tf_op jit(solution)/shard_map/chunk_back/pallas_call | solution.py:353
  31.8 1.6 %collective-permute-start.12 = (bf16[16,1024]{1,0:T(8,128)(2,1)S(1)}, bf16[16,1024]{1,0:T(8,128)(2,1)S(1)}, u32[]{:S(2)}, u32[]{:S(2)}) collective-permute-start(bf16[16,1024]{1,0:T(8,128)(2,1)S(1)} %get-tuple-element.87), channel_id=1, source_target_pairs={{0,1},{1,2},{2,3},{3,0},{4,5},{5,6},{6,7},{7,4},{8,9},{9,10},{10,1... | collective-permute-start | bytes 98312 | tf_op jit(solution)/shard_map/ppermute | solution.py:38
  33.4 2.6 %collective-permute-start.13 = (bf16[16,1024]{1,0:T(8,128)(2,1)S(1)}, bf16[16,1024]{1,0:T(8,128)(2,1)S(1)}, u32[]{:S(2)}, u32[]{:S(2)}) collective-permute-start(bf16[16,1024]{1,0:T(8,128)(2,1)S(1)} %get-tuple-element.88), channel_id=1, source_target_pairs={{0,2},{1,3},{2,0},{3,1},{4,6},{5,7},{6,4},{7,5},{8,10},{9,11},{10,... | collective-permute-start | bytes 98312 | tf_op jit(solution)/shard_map/ppermute | solution.py:38
  36.0 1.3 %collective-permute-start.14 = (bf16[16,1024]{1,0:T(8,128)(2,1)S(1)}, bf16[16,1024]{1,0:T(8,128)(2,1)S(1)}, u32[]{:S(2)}, u32[]{:S(2)}) collective-permute-start(bf16[16,1024]{1,0:T(8,128)(2,1)S(1)} %get-tuple-element.89), channel_id=1, source_target_pairs={{0,3},{1,0},{2,1},{3,2},{4,7},{5,4},{6,5},{7,6},{8,11},{9,8},{10,9... | collective-permute-start | bytes 98312 | tf_op jit(solution)/shard_map/ppermute | solution.py:38
  37.4 1.6 %chunk_finish.1 = (bf16[128,4096]{1,0:T(8,128)(2,1)}, f32[128,1024]{1,0:T(8,128)S(1)}, bf16[64,128]{1,0:T(8,128)(2,1)}, bf16[128,1024]{1,0:T(8,128)(2,1)}) custom-call(bf16[128,4096]{1,0:T(8,128)(2,1)S(1)} %bitcast.20, bf16[64,128]{1,0:T(8,128)(2,1)S(1)} %bitcast.35, ...), custom_call_target="tpu_custom_call", output_to_operand_aliasing={{0}: (8, {}), {1}: (9, {})} | custom-call | flops 167772160 | bytes 1048576 | tf_op jit(solution)/shard_map/chunk_finish/pallas_call | solution.py:353
  39.0 1.0 %collective-permute-done.14 = bf16[16,1024]{1,0:T(8,128)(2,1)S(1)} collective-permute-done((bf16[16,1024]{1,0:T(8,128)(2,1)S(1)}, bf16[16,1024]{1,0:T(8,128)(2,1)S(1)}, u32[]{:S(2)}, u32[]{:S(2)}) %collective-permute-start.14) | collective-permute-done | bytes 32800 | tf_op jit(solution)/shard_map/ppermute | solution.py:38
  39.9 0.6 %add_bitcast_fusion = f32[1,16,1024]{2,1,0:T(8,128)} fusion(bf16[16,1024]{1,0:T(8,128)(2,1)S(1)} %collective-permute-done.14, bf16[16,1024]{1,0:T(8,128)(2,1)S(1)} %collective-permute-done.13, bf16[16,1024]{1,0:T(8,128)(2,1)S(1)} %collective-permute-done.12, bf16[16,1024]{1,0:T(8,128)(2,1)S(1)} %get-tuple-element.86), kind=kLoop, calls=%fused_computation.1 | loop fusion | flops 114688 | bytes 196608 | tf_op jit(solution)/shard_map/broadcast_in_dim | solution.py:490
  (21 shorter events, 0.2 us)
Async XLA Ops:
  1.6 10.1 %collective-permute-start.1 = (bf16[128,1024]{1,0:T(8,128)(2,1)S(1)}, bf16[128,1024]{1,0:T(8,128)(2,1)S(1)}, u32[]{:S(2)}, u32[]{:S(2)}) collective-permute-start(bf16[128,1024]{1,0:T(8,128)(2,1)S(1)} %split_piece.3.rest_0_), channel_id=1, source_target_pairs={{0,16},{16,0},{1,17},{17,1},{2,18},{18,2},{3,19},{19,3},{4,20},{20... | collective-permute-start | bytes 786440 | tf_op jit(solution)/shard_map/ppermute | solution.py:38
  5.7 10.9 %collective-permute-start = (bf16[128,1024]{1,0:T(8,128)(2,1)S(1)}, bf16[128,1024]{1,0:T(8,128)(2,1)S(1)}, u32[]{:S(2)}, u32[]{:S(2)}) collective-permute-start(bf16[128,1024]{1,0:T(8,128)(2,1)S(1)} %get-tuple-element.47), channel_id=1, source_target_pairs={{0,4},{4,8},{8,12},{12,0},{1,5},{5,9},{9,13},{13,1},{2,6},{6,10},{... | collective-permute-start | bytes 786440 | tf_op jit(solution)/shard_map/ppermute | solution.py:38
  5.8 13.7 %collective-permute-start.3 = (bf16[128,1024]{1,0:T(8,128)(2,1)S(1)}, bf16[128,1024]{1,0:T(8,128)(2,1)S(1)}, u32[]{:S(2)}, u32[]{:S(2)}) collective-permute-start(bf16[128,1024]{1,0:T(8,128)(2,1)S(1)} %get-tuple-element.49), channel_id=1, source_target_pairs={{0,16},{16,0},{1,17},{17,1},{2,18},{18,2},{3,19},{19,3},{4,20},{20... | collective-permute-start | bytes 786440 | tf_op jit(solution)/shard_map/ppermute | solution.py:38
  5.9 0.7 %copy-start.3 = (s32[1,1,512]{2,1,0:T(1,128)S(1)}, s32[1,1,512]{2,1,0:T(1,128)}, u32[]{:S(2)}) copy-start(s32[1,1,512]{2,1,0:T(1,128)} %param.11) | copy-start | bytes 6148
  6.8 9.9 %copy-start = (bf16[1,1,128,4096]{3,2,1,0:T(8,128)(2,1)S(1)}, bf16[1,1,128,4096]{3,2,1,0:T(8,128)(2,1)}, u32[]{:S(2)}) copy-start(bf16[1,1,128,4096]{3,2,1,0:T(8,128)(2,1)} %param.6) | copy-start | bytes 3145732
  11.8 4.9 %copy-start.2 = (bf16[1,1,128,64]{2,3,1,0:T(8,128)(2,1)S(1)}, bf16[1,1,128,64]{2,3,1,0:T(8,128)(2,1)}, u32[]{:S(2)}) copy-start(bf16[1,1,128,64]{2,3,1,0:T(8,128)(2,1)} %param.8) | copy-start | bytes 49156
  12.8 3.9 %copy-start.1 = (bf16[1,1,128,1024]{3,2,1,0:T(8,128)(2,1)S(1)}, bf16[1,1,128,1024]{3,2,1,0:T(8,128)(2,1)}, u32[]{:S(2)}) copy-start(bf16[1,1,128,1024]{3,2,1,0:T(8,128)(2,1)} %param.7) | copy-start | bytes 786436
  12.8 6.7 %collective-permute-start.2 = (bf16[64,1024]{1,0:T(8,128)(2,1)S(1)}, bf16[64,1024]{1,0:T(8,128)(2,1)S(1)}, u32[]{:S(2)}, u32[]{:S(2)}) collective-permute-start(bf16[64,1024]{1,0:T(8,128)(2,1)S(1)} %get-tuple-element.48.refs_5_), channel_id=1, source_target_pairs={{0,8},{4,12},{8,0},{12,4},{1,9},{5,13},{9,1},{13,5},{2,10},{6,14},... | collective-permute-start | bytes 393224 | tf_op jit(solution)/shard_map/ppermute | solution.py:38
  14.9 10.1 %collective-permute-start.7 = (bf16[128,1024]{1,0:T(8,128)(2,1)S(1)}, bf16[128,1024]{1,0:T(8,128)(2,1)S(1)}, u32[]{:S(2)}, u32[]{:S(2)}) collective-permute-start(bf16[128,1024]{1,0:T(8,128)(2,1)S(1)} %get-tuple-element.57), channel_id=1, source_target_pairs={{0,16},{16,0},{1,17},{17,1},{2,18},{18,2},{3,19},{19,3},{4,20},{20... | collective-permute-start | bytes 786440 | tf_op jit(solution)/shard_map/ppermute | solution.py:38
  16.5 7.0 %collective-permute-start.6 = (bf16[64,1024]{1,0:T(8,128)(2,1)S(1)}, bf16[64,1024]{1,0:T(8,128)(2,1)S(1)}, u32[]{:S(2)}, u32[]{:S(2)}) collective-permute-start(bf16[64,1024]{1,0:T(8,128)(2,1)S(1)} %get-tuple-element.48.refs_5_), channel_id=1, source_target_pairs={{0,12},{4,0},{8,4},{12,8},{1,13},{5,1},{9,5},{13,9},{2,14},{6,2},{... | collective-permute-start | bytes 393224 | tf_op jit(solution)/shard_map/ppermute | solution.py:38
  18.8 6.3 %collective-permute-start.8 = (bf16[64,1024]{1,0:T(8,128)(2,1)S(1)}, bf16[64,1024]{1,0:T(8,128)(2,1)S(1)}, u32[]{:S(2)}, u32[]{:S(2)}) collective-permute-start(bf16[64,1024]{1,0:T(8,128)(2,1)S(1)} %get-tuple-element.64), channel_id=1, source_target_pairs={{0,12},{4,0},{8,4},{12,8},{1,13},{5,1},{9,5},{13,9},{2,14},{6,2},{... | collective-permute-start | bytes 393224 | tf_op jit(solution)/shard_map/ppermute | solution.py:38
  19.4 7.4 %collective-permute-start.5 = (bf16[64,1024]{1,0:T(8,128)(2,1)S(1)}, bf16[64,1024]{1,0:T(8,128)(2,1)S(1)}, u32[]{:S(2)}, u32[]{:S(2)}) collective-permute-start(bf16[64,1024]{1,0:T(8,128)(2,1)S(1)} %get-tuple-element.56), channel_id=1, source_target_pairs={{0,16},{16,0},{1,17},{17,1},{2,18},{18,2},{3,19},{19,3},{4,20},{20... | collective-permute-start | bytes 393224 | tf_op jit(solution)/shard_map/ppermute | solution.py:38
  21.6 5.6 %collective-permute-start.9 = (bf16[64,1024]{1,0:T(8,128)(2,1)S(1)}, bf16[64,1024]{1,0:T(8,128)(2,1)S(1)}, u32[]{:S(2)}, u32[]{:S(2)}) collective-permute-start(bf16[64,1024]{1,0:T(8,128)(2,1)S(1)} %get-tuple-element.70), channel_id=1, source_target_pairs={{0,8},{4,12},{8,0},{12,4},{1,9},{5,13},{9,1},{13,5},{2,10},{6,14},... | collective-permute-start | bytes 393224 | tf_op jit(solution)/shard_map/ppermute | solution.py:38
  23.6 6.7 %collective-permute-start.4 = (bf16[64,1024]{1,0:T(8,128)(2,1)S(1)}, bf16[64,1024]{1,0:T(8,128)(2,1)S(1)}, u32[]{:S(2)}, u32[]{:S(2)}) collective-permute-start(bf16[64,1024]{1,0:T(8,128)(2,1)S(1)} %get-tuple-element.55), channel_id=1, source_target_pairs={{0,16},{16,0},{1,17},{17,1},{2,18},{18,2},{3,19},{19,3},{4,20},{20... | collective-permute-start | bytes 393224 | tf_op jit(solution)/shard_map/ppermute | solution.py:38
  26.7 4.4 %collective-permute-start.11 = (bf16[64,1024]{1,0:T(8,128)(2,1)S(1)}, bf16[64,1024]{1,0:T(8,128)(2,1)S(1)}, u32[]{:S(2)}, u32[]{:S(2)}) collective-permute-start(bf16[64,1024]{1,0:T(8,128)(2,1)S(1)} %get-tuple-element.79), channel_id=1, source_target_pairs={{0,4},{4,8},{8,12},{12,0},{1,5},{5,9},{9,13},{13,1},{2,6},{6,10},{... | collective-permute-start | bytes 393224 | tf_op jit(solution)/shard_map/ppermute | solution.py:38
  28.9 8.5 %collective-permute-start.10 = (bf16[64,1024]{1,0:T(8,128)(2,1)S(1)}, bf16[64,1024]{1,0:T(8,128)(2,1)S(1)}, u32[]{:S(2)}, u32[]{:S(2)}) collective-permute-start(bf16[64,1024]{1,0:T(8,128)(2,1)S(1)} %get-tuple-element.71), channel_id=1, source_target_pairs={{0,12},{4,0},{8,4},{12,8},{1,13},{5,1},{9,5},{13,9},{2,14},{6,2},{... | collective-permute-start | bytes 393224 | tf_op jit(solution)/shard_map/ppermute | solution.py:38
  31.8 7.2 %collective-permute-start.12 = (bf16[16,1024]{1,0:T(8,128)(2,1)S(1)}, bf16[16,1024]{1,0:T(8,128)(2,1)S(1)}, u32[]{:S(2)}, u32[]{:S(2)}) collective-permute-start(bf16[16,1024]{1,0:T(8,128)(2,1)S(1)} %get-tuple-element.87), channel_id=1, source_target_pairs={{0,1},{1,2},{2,3},{3,0},{4,5},{5,6},{6,7},{7,4},{8,9},{9,10},{10,1... | collective-permute-start | bytes 98312 | tf_op jit(solution)/shard_map/ppermute | solution.py:38
  33.4 5.5 %collective-permute-start.13 = (bf16[16,1024]{1,0:T(8,128)(2,1)S(1)}, bf16[16,1024]{1,0:T(8,128)(2,1)S(1)}, u32[]{:S(2)}, u32[]{:S(2)}) collective-permute-start(bf16[16,1024]{1,0:T(8,128)(2,1)S(1)} %get-tuple-element.88), channel_id=1, source_target_pairs={{0,2},{1,3},{2,0},{3,1},{4,6},{5,7},{6,4},{7,5},{8,10},{9,11},{10,... | collective-permute-start | bytes 98312 | tf_op jit(solution)/shard_map/ppermute | solution.py:38
  36.0 3.9 %collective-permute-start.14 = (bf16[16,1024]{1,0:T(8,128)(2,1)S(1)}, bf16[16,1024]{1,0:T(8,128)(2,1)S(1)}, u32[]{:S(2)}, u32[]{:S(2)}) collective-permute-start(bf16[16,1024]{1,0:T(8,128)(2,1)S(1)} %get-tuple-element.89), channel_id=1, source_target_pairs={{0,3},{1,0},{2,1},{3,2},{4,7},{5,4},{6,5},{7,6},{8,11},{9,8},{10,9... | collective-permute-start | bytes 98312 | tf_op jit(solution)/shard_map/ppermute | solution.py:38
